TPU v7x, 32 devices: a whole 2x2x4 slice. The times are simulated.
32 devices in a mesh: merge: 4 (over z), row: 4 (over x, core), col: 2 (over y).
Axes of the slice: x: 2, y: 2, z: 4, core: 2. Of those that a mesh axis runs over, the one named last changes fastest.
Arguments:
- eigen_rows: bfloat16 [4, 128, 16384], P('merge', 'row', 'col'), may hold values from -6 to 6
- live_one: int32 [4], replicated, may hold values from 2048 to 6144, as said below
- order_one: int32 [4, 16384], P('merge'), may hold values from 0 to 16383, each once within a row
- poles_one: float32 [4, 16384], P('merge'), may hold values from -2048 to 2048.3, as said below
- weights_one: float32 [4, 16384], P('merge'), may hold values from 0.003 to 32, as said below
- roots_one: float32 [4, 16384], P('merge'), may hold values from -2047.55 to 2048.85, as said below
- live_two: int32 [4], replicated, may hold values from 2048 to 6144, as said below
- order_two: int32 [4, 16384], P('merge'), may hold values from 0 to 16383, each once within a row
- poles_two: float32 [4, 16384], P('merge'), may hold values from -2048 to 2048.3, as said below
- weights_two: float32 [4, 16384], P('merge'), may hold values from 0.003 to 32, as said below
- roots_two: float32 [4, 16384], P('merge'), may hold values from -2047.55 to 2048.85, as said below
Outputs:
- vectors_two: bfloat16 [4, 128, 32768], P('merge', 'row', 'col')
Inputs may be any that keep to these rules, and one draw needn't show every extreme that they name: `live_one`: both ends of the range are reached in every draw. `live_two`: both ends of the range are reached in every draw. `weights_one`: Positive. `weights_two`: Positive. `poles_one`: every offset minus its floor lies in [0, 0.3]. `roots_one`: every offset minus its floor lies in [0.45, 0.85], so every root stays 0.15 or more from every pole. `poles_two`: every offset minus its floor lies in [0, 0.3]. `roots_two`: every offset minus its floor lies in [0.45, 0.85], so every root stays 0.15 or more from every pole.
All inputs are finite; a program needn't handle non-finite values.
Results may differ from a plain program's by a relative error of at most 0.0031.
Values may be sent and summed in bfloat16 or wider, within the bound.
A program may use at most 64 MiB of HBM per device.

v0:
```python
import functools

import jax
import jax.numpy as jnp
from jax import lax
from jax.experimental import pallas as pl
from jax.experimental.pallas import tpu as pltpu
from jax.sharding import PartitionSpec as P

LANE = 128
POLE_TILE = 512
VMEM_LIMIT = 56 * 1024 * 1024
MESH = pl.DeviceIdType.MESH


def inverse_of(distance):
    guess = pl.reciprocal(distance, approx=True)
    return guess * (2.0 - distance * guess)


def spec(space):
    return pl.BlockSpec(memory_space=space)


def fill_table(source_ref, table_ref, start=0):
    rows, width = source_ref.shape
    blocks = width // LANE
    unroll = max(k for k in (8, 6, 4, 3, 2, 1) if blocks % k == 0)

    def some(turn, carry):
        for k in range(unroll):
            opening = pl.multiple_of((turn * unroll + k) * LANE, LANE)
            block = source_ref[:, pl.ds(opening, LANE)].astype(jnp.float32)
            table_ref[pl.ds(start + opening, LANE), 0:rows] = block.T
        return carry

    lax.fori_loop(0, blocks // unroll, some, 0)


def pick_block(table_ref, stage_ref, index_of, rows):
    for k in range(LANE):
        stage_ref[k : k + 1, :] = table_ref[pl.ds(index_of(k), 1), :]
    return stage_ref[...].T[0:rows, :].astype(jnp.bfloat16)


def pick_one_kernel(info_ref, order_ref, source_ref, out_ref, table_ref, stage_ref):
    rows = source_ref.shape[0]
    table_ref[...] = jnp.zeros(table_ref.shape, jnp.float32)
    fill_table(source_ref, table_ref)
    out_ref[...] = jnp.zeros(out_ref.shape, out_ref.dtype)
    first, live = info_ref[0], info_ref[1]
    count = jnp.clip((live - first + LANE - 1) // LANE, 0, out_ref.shape[1] // LANE)

    def one(step, carry):
        opening = pl.multiple_of(step * LANE, LANE)
        out_ref[:, pl.ds(opening, LANE)] = pick_block(
            table_ref, stage_ref, lambda k: order_ref[first + opening + k], rows
        )
        return carry

    lax.fori_loop(0, count, one, 0)


def pick_one(info, order, source, width):
    rows, total = source.shape
    return pl.pallas_call(
        pick_one_kernel,
        out_shape=(
            jax.ShapeDtypeStruct((rows, width), jnp.bfloat16),
            jax.ShapeDtypeStruct((total, LANE), jnp.float32),
        ),
        in_specs=[spec(pltpu.SMEM), spec(pltpu.SMEM), spec(pltpu.VMEM)],
        out_specs=(spec(pltpu.VMEM), spec(pltpu.VMEM)),
        scratch_shapes=[pltpu.VMEM((LANE, LANE), jnp.float32)],
        compiler_params=pltpu.CompilerParams(vmem_limit_bytes=VMEM_LIMIT),
    )(info, order, source)


def pick_two_kernel(
    stride,
    info_ref,
    order_ref,
    place_ref,
    level_ref,
    source_ref,
    out_ref,
    moved_ref,
    table_ref,
    stage_ref,
    copy_sem,
):
    group, rows, width = level_ref.shape
    wide = group * width
    copy = pltpu.make_async_copy(
        source_ref, table_ref.at[pl.ds(wide, source_ref.shape[0])], copy_sem
    )
    copy.start()
    out_ref[...] = jnp.zeros(out_ref.shape, out_ref.dtype)
    moved_ref[...] = jnp.zeros(moved_ref.shape, moved_ref.dtype)
    table_ref[0:wide, :] = jnp.zeros((wide, LANE), jnp.float32)
    for part in range(group):
        fill_table(level_ref.at[part], table_ref, part * width)
    copy.wait()
    first, live = info_ref[0], info_ref[1]
    count = jnp.clip((live - first + LANE - 1) // LANE, 0, out_ref.shape[1] // LANE)

    def one(step, carry):
        opening = pl.multiple_of(step * LANE, LANE)
        out_ref[:, pl.ds(opening, LANE)] = pick_block(
            table_ref, stage_ref, lambda k: place_ref[order_ref[first + opening + k]], rows
        )
        return carry

    lax.fori_loop(0, count, one, 0)
    offset, low, high = info_ref[2], info_ref[3], info_ref[4]

    def other(step, carry):
        opening = pl.multiple_of(step * LANE, LANE)
        begin = offset + step * stride
        moved_ref[:, pl.ds(opening, LANE)] = pick_block(
            table_ref, stage_ref, lambda k: place_ref[order_ref[begin + k]], rows
        )
        return carry

    lax.fori_loop(low, high, other, 0)


def pick_two(stride, info, order, place, level, table, width, moved_width):
    group, rows, wide = level.shape
    wide = wide * group
    return pl.pallas_call(
        functools.partial(pick_two_kernel, stride),
        out_shape=(
            jax.ShapeDtypeStruct((rows, width), jnp.bfloat16),
            jax.ShapeDtypeStruct((rows, moved_width), jnp.bfloat16),
        ),
        in_specs=[spec(pltpu.SMEM)] * 3 + [spec(pltpu.VMEM), spec(pl.ANY)],
        out_specs=(spec(pltpu.VMEM), spec(pltpu.VMEM)),
        scratch_shapes=[
            pltpu.VMEM((table.shape[0] + wide, LANE), jnp.float32),
            pltpu.VMEM((LANE, LANE), jnp.float32),
            pltpu.SemaphoreType.DMA,
        ],
        compiler_params=pltpu.CompilerParams(vmem_limit_bytes=VMEM_LIMIT),
    )(info, order, place, level, table)


def wide_columns(values):
    width = 2 * LANE if values.shape[0] % 2 == 0 else LANE
    return values.reshape(-1, width)


def across(values, width):
    return jnp.concatenate([values] * (width // LANE), axis=1)


def quotients(start, rows, stride, half, shift_ref, weight_ref, place, root):
    width = place.shape[1]
    slot = lax.broadcasted_iota(jnp.int32, (rows, LANE), 0) + start
    poles = across((slot * stride + half).astype(jnp.float32), width)
    shifts = across(shift_ref[pl.ds(start, rows), :], width)
    distance = (poles - place) + (shifts - root)
    return across(weight_ref[pl.ds(start, rows), :], width) * inverse_of(distance)


def norm_kernel(stride, info_ref, shift_ref, weight_ref, place_ref, root_ref, out_ref):
    live, half, blocks = info_ref[0], info_ref[1], info_ref[2]
    tiles = (live + POLE_TILE - 1) // POLE_TILE
    width = place_ref.shape[1]
    turns = (blocks * LANE + width - 1) // width
    out_ref[...] = jnp.ones(out_ref.shape, jnp.float32)

    def one_block(block, carry):
        place = place_ref[pl.ds(block, 1), :]
        root = root_ref[pl.ds(block, 1), :]

        def one_tile(tile, running):
            opening = pl.multiple_of(tile * POLE_TILE, POLE_TILE)
            for part in range(POLE_TILE // 32):
                term = quotients(
                    opening + part * 32, 32, stride, half, shift_ref, weight_ref, place, root
                )
                running = running + jnp.sum((term * term).reshape(4, 8, width), axis=0)
            return running

        sums = lax.fori_loop(0, tiles, one_tile, jnp.zeros((8, width), jnp.float32))
        out_ref[pl.ds(block, 1), :] = jnp.sum(sums, axis=0, keepdims=True)
        return carry

    lax.fori_loop(0, turns, one_block, 0)


def column_norms(stride, info, shift, weight, place, root):
    work = shift.shape[0] * place.size
    return pl.pallas_call(
        functools.partial(norm_kernel, stride),
        out_shape=jax.ShapeDtypeStruct(place.shape, jnp.float32),
        in_specs=[spec(pltpu.SMEM)] + [spec(pltpu.VMEM)] * 4,
        out_specs=spec(pltpu.VMEM),
        cost_estimate=pl.CostEstimate(
            flops=3000 * work, bytes_accessed=8 * work, transcendentals=work
        ),
        compiler_params=pltpu.CompilerParams(vmem_limit_bytes=VMEM_LIMIT),
    )(info, shift, weight, place, root)


def apply_kernel(
    stride, info_ref, rows_ref, shift_ref, weight_ref, place_ref, root_ref, inverse_ref, out_ref
):
    live, half, blocks = info_ref[0], info_ref[1], info_ref[2]
    tiles = (live + POLE_TILE - 1) // POLE_TILE
    row_total = rows_ref.shape[0]
    width = place_ref.shape[1]
    turns = (blocks * LANE + width - 1) // width
    out_ref[...] = jnp.zeros(out_ref.shape, out_ref.dtype)

    def one_block(block, carry):
        place = place_ref[pl.ds(block, 1), :]
        root = root_ref[pl.ds(block, 1), :]
        inverse = inverse_ref[pl.ds(block, 1), :]

        def one_tile(tile, running):
            opening = pl.multiple_of(tile * POLE_TILE, POLE_TILE)
            pieces = []
            for part in range(POLE_TILE // 32):
                term = quotients(
                    opening + part * 32, 32, stride, half, shift_ref, weight_ref, place, root
                )
                pieces.append((term * inverse).astype(jnp.bfloat16))
            return running + jnp.dot(
                rows_ref[:, pl.ds(opening, POLE_TILE)],
                jnp.concatenate(pieces, axis=0),
                preferred_element_type=jnp.float32,
            )

        total = lax.fori_loop(0, tiles, one_tile, jnp.zeros((row_total, width), jnp.float32))
        out_ref[:, pl.ds(pl.multiple_of(block * width, width), width)] = total.astype(
            out_ref.dtype
        )
        return carry

    lax.fori_loop(0, turns, one_block, 0)


def cauchy_product(stride, info, rows, shift, weight, place, root, inverse):
    return pl.pallas_call(
        functools.partial(apply_kernel, stride),
        out_shape=jax.ShapeDtypeStruct((rows.shape[0], place.size), jnp.bfloat16),
        in_specs=[spec(pltpu.SMEM)] + [spec(pltpu.VMEM)] * 6,
        out_specs=spec(pltpu.VMEM),
        cost_estimate=pl.CostEstimate(
            flops=3000 * shift.shape[0] * place.size, bytes_accessed=0, transcendentals=0
        ),
        compiler_params=pltpu.CompilerParams(vmem_limit_bytes=VMEM_LIMIT),
    )(info, rows, shift, weight, place, root, inverse)


def ceil_to(value, unit):
    return (value + unit - 1) // unit * unit


def own_blocks(values, group, member):
    spread = values.reshape(-1, group, LANE)
    return lax.dynamic_index_in_dim(spread, member, 1, keepdims=False)


def block_share(live, group, member):
    total = (live + LANE - 1) // LANE
    return jnp.maximum((total - member + group - 1) // group, 0)


def exchange_kernel(
    row_count, col_count, in_place, source_ref, out_ref, send_sem, recv_sem, own_sem
):
    merge = lax.axis_index("merge")
    row, col = lax.axis_index("row"), lax.axis_index("col")
    group = row_count * col_count
    me = row * col_count + col
    others = []
    for k in range(1, group):
        peer = lax.rem(me + k, group)
        others.append((merge, peer // col_count, lax.rem(peer, col_count)))
    barrier = pltpu.get_barrier_semaphore()
    for device in others:
        pl.semaphore_signal(barrier, inc=1, device_id=device, device_id_type=MESH)
    pl.semaphore_wait(barrier, group - 1)
    if in_place:
        rows, width = source_ref.shape
        target = out_ref.at[
            pl.ds(pl.multiple_of(row * rows, rows), rows),
            pl.ds(pl.multiple_of(col * width, width), width),
        ]
    else:
        target = out_ref.at[me]
    copies = []
    for k, device in enumerate(others):
        copy = pltpu.make_async_remote_copy(
            src_ref=source_ref if in_place else source_ref.at[device[1]],
            dst_ref=target,
            send_sem=send_sem.at[k],
            recv_sem=recv_sem.at[k],
            device_id=device,
            device_id_type=MESH,
        )
        copy.start()
        copies.append(copy)
    own = pltpu.make_async_copy(source_ref if in_place else source_ref.at[row], target, own_sem)
    own.start()
    own.wait()
    for copy in copies:
        copy.wait()


def exchange(source, in_place, number):
    row_count, col_count = lax.axis_size("row"), lax.axis_size("col")
    group = row_count * col_count
    rows, width = source.shape[-2:]
    shape = (row_count * rows, col_count * width) if in_place else (group, rows, width)
    return pl.pallas_call(
        functools.partial(exchange_kernel, row_count, col_count, in_place),
        out_shape=jax.ShapeDtypeStruct(shape, source.dtype),
        in_specs=[spec(pl.ANY)],
        out_specs=spec(pl.ANY),
        scratch_shapes=[
            pltpu.SemaphoreType.DMA((group - 1,)),
            pltpu.SemaphoreType.DMA((group - 1,)),
            pltpu.SemaphoreType.DMA,
        ],
        compiler_params=pltpu.CompilerParams(collective_id=number, has_side_effects=True),
    )(source)


def join_columns(piece, number):
    row_count = lax.axis_size("row")
    return exchange(piece.reshape(row_count, -1, piece.shape[1]), False, number)


def spread_moved(moved):
    col_count, col_index = lax.axis_size("col"), lax.axis_index("col")
    rows, width = moved.shape
    parts = moved.reshape(rows, col_count, width // col_count)
    pieces = jnp.zeros((col_count, rows, width // col_count), moved.dtype)
    for k in range(col_count):
        part = lax.dynamic_index_in_dim(parts, (col_index + k) % col_count, 1, keepdims=False)
        if k:
            pairs = [(c, (c + k) % col_count) for c in range(col_count)]
            part = lax.ppermute(part, "col", pairs)
        pieces = lax.dynamic_update_index_in_dim(
            pieces, part, (col_index - k + col_count) % col_count, 0
        )
    pieces = pieces.reshape(col_count, rows, -1, LANE)
    return jnp.transpose(pieces, (1, 2, 0, 3)).reshape(rows, width)


def spread_poles(values, live, limit, masked):
    values = values[:limit]
    if masked:
        values = jnp.where(jnp.arange(limit, dtype=jnp.int32) < live, values, 0.0)
    return jnp.broadcast_to(values[:, None], (limit, LANE))


def shards(
    eigen_rows,
    live_one,
    order_one,
    poles_one,
    weights_one,
    roots_one,
    live_two,
    order_two,
    poles_two,
    weights_two,
    roots_two,
):
    col_count, row_count = lax.axis_size("col"), lax.axis_size("row")
    col_index, row_index = lax.axis_index("col"), lax.axis_index("row")
    merge_index = lax.axis_index("merge")
    merge_order = order_one.shape[1]
    group, member = row_count * col_count, row_index * col_count + col_index
    most = 3 * merge_order // 8
    pole_limit = ceil_to(most, max(POLE_TILE, LANE * col_count))
    share = pole_limit // col_count
    wide_one = ceil_to(most, LANE * group)
    wide_two = ceil_to(2 * most, LANE * group)
    out_width = 2 * merge_order // col_count
    zero = jnp.zeros((), jnp.int32)

    half = merge_index % 2
    pair_first = merge_index - half
    count_first, count_second = live_two[pair_first], live_two[pair_first + 1]
    count_own = live_two[merge_index]
    joined = count_first + count_second
    pairs = [(k, k ^ 1) for k in range(lax.axis_size("merge"))]
    own_roots = roots_two[0, :most]
    other_roots = lax.ppermute(own_roots, "merge", pairs)
    roots_first = jnp.where(half == 0, own_roots, other_roots)
    roots_second = jnp.where(half == 0, other_roots, own_roots)
    columns = jnp.arange(wide_two, dtype=jnp.int32)
    from_first = columns < count_first
    padded_first = jnp.concatenate([roots_first, jnp.zeros((wide_two - most,), jnp.float32)])
    padded_second = jnp.concatenate(
        [jnp.zeros((most,), jnp.float32), roots_second, jnp.zeros((wide_two,), jnp.float32)]
    )
    moved_second = lax.dynamic_slice_in_dim(padded_second, most - count_first, wide_two)
    root_shift = jnp.where(from_first, padded_first, moved_second)
    root_shift = jnp.where(columns < joined, root_shift, 0.5)
    root_place = jnp.where(from_first, 2 * columns, 2 * (columns - count_first) + 1)
    root_place = wide_columns(own_blocks(root_place.astype(jnp.float32), group, member))
    root_shift = wide_columns(own_blocks(root_shift, group, member))
    blocks_two = block_share(joined, group, member)
    info_two = jnp.stack([count_own, half, blocks_two]).astype(jnp.int32)
    shift_two = spread_poles(poles_two[0], count_own, pole_limit, False)
    weight_two = spread_poles(weights_two[0], count_own, pole_limit, True)
    sums_two = column_norms(2, info_two, shift_two, weight_two, root_place, root_shift)
    sums_two = sums_two + lax.ppermute(sums_two, "merge", pairs)

    live = live_one[merge_index]
    first = col_index * share
    gathered = lax.all_gather(eigen_rows[0], "col", axis=1, tiled=True)
    column_one = jnp.arange(wide_one, dtype=jnp.int32).astype(jnp.float32)
    place_one = wide_columns(own_blocks(column_one, group, member))
    root_one = wide_columns(own_blocks(roots_one[0, :wide_one], group, member))
    info_one = jnp.stack([live, zero, block_share(live, group, member)]).astype(jnp.int32)
    shift_one = spread_poles(poles_one[0], live, pole_limit, False)
    weight_one = spread_poles(weights_one[0], live, pole_limit, True)
    sums_one = column_norms(1, info_one, shift_one, weight_one, place_one, root_one)
    inverse_one = 1.0 / jnp.sqrt(sums_one)
    inverse_two = 1.0 / jnp.sqrt(sums_two)
    gathered, inverse_one, inverse_two, weight_one, weight_two = lax.optimization_barrier(
        (gathered, inverse_one, inverse_two, weight_one, weight_two)
    )
    picked, table = pick_one(jnp.stack([first, live]).astype(jnp.int32), order_one[0], gathered, share)
    rows_one = exchange(picked, True, 0)
    level = cauchy_product(
        1, info_one, rows_one, shift_one, weight_one, place_one, root_one, inverse_one
    )
    level = join_columns(level, 1)

    slots = jnp.arange(merge_order, dtype=jnp.int32)
    slot_block = slots // LANE
    level_place = (slot_block % group * (wide_one // group // LANE) + slot_block // group) * LANE
    place = jnp.where(slots < live, level_place + slots % LANE, wide_one + order_one[0])
    offset = jnp.where(half == 0, -count_second, -merge_order)
    low = jnp.where(half == 0, joined, merge_order + count_second)
    high = jnp.where(half == 0, merge_order + count_second, 2 * merge_order)
    low_block, high_block = low // LANE, (high + LANE - 1) // LANE
    low_turn = (low_block - col_index + col_count - 1) // col_count
    high_turn = (high_block - col_index + col_count - 1) // col_count
    info_pick = jnp.stack(
        [first, count_own, offset + col_index * LANE, low_turn, high_turn]
    ).astype(jnp.int32)
    order_pad = jnp.pad(order_two[0], (0, LANE))
    picked, moved = pick_two(
        col_count * LANE, info_pick, order_pad, place, level, table, share, out_width
    )
    rows_two = exchange(picked, True, 2)
    mixed = cauchy_product(
        2,
        info_two,
        rows_two,
        shift_two,
        weight_two,
        root_place,
        root_shift,
        inverse_two,
    )
    mixed = join_columns(mixed, 3)
    rows = mixed.shape[1]
    mixed = mixed.reshape(group, rows, -1, LANE)
    mixed = jnp.transpose(mixed, (1, 2, 0, 3)).reshape(rows, wide_two)
    mixed = jnp.pad(mixed, ((0, 0), (0, 2 * merge_order - wide_two)))
    begin = col_index * out_width
    mixed = lax.dynamic_slice_in_dim(mixed, begin, out_width, 1)
    own = jnp.arange(out_width, dtype=jnp.int32) + begin
    keep = (own >= low) & (own < high)
    moved = jnp.where(keep[None, :], spread_moved(moved), jnp.zeros((), jnp.bfloat16))
    result = jnp.where((own < joined)[None, :], mixed, moved)
    return result[None]


def solution(mesh):
    placed = (
        P("merge", "row", "col"),
        P(),
        P("merge", None),
        P("merge", None),
        P("merge", None),
        P("merge", None),
        P(),
        P("merge", None),
        P("merge", None),
        P("merge", None),
        P("merge", None),
    )
    return jax.shard_map(
        shards, mesh=mesh, in_specs=placed, out_specs=P("merge", "row", "col"), check_vma=False
    )
```

profile of v0, /device:TPU:0, one launch (start us, length us, event | category | flops | bytes accessed | tf_op | source)
XLA Modules:
  0.0 234.6 jit_solution(8769572552521415712)
XLA Ops:
  6.5 0.0 slice-start.1
  6.5 0.0 all-gather.3.cloned.1.call-start
  6.5 0.8 slice.33
  7.3 3.0 %collective-permute-start = (f32[6144]{0:T(1024)S(1)}, f32[6144]{0:T(1024)S(1)}, u32[]{:S(2)}, u32[]{:S(2)}) collective-permute-start(f32[6144]{0:T(1024)S(1)} %bitcast.68), channel_id=1, source_target_pairs={{0,8},{8,0},{16,24},{24,16},{1,9},{9,1},{17,25},{25,17},{2,10},{10... | collective-permute-start | bytes 73736 | tf_op jit(solution)/shard_map/ppermute | solution.py:395
  10.3 0.0 all-gather.3.cloned.1.call-update
  10.4 1.3 dynamic_slice.42
  12.5 1.4 fusion.35
  15.8 0.7 slice.31
  16.6 0.7 slice.29
  17.3 0.6 reshape.84.root_ref
  17.9 0.6 reshape.83.place_ref
  18.5 0.7 slice.27
  19.3 0.7 fusion.31
  20.0 2.2 fusion.13.place_ref
  22.2 0.6 fusion.32
  22.9 0.6 select_convert_fusion
  23.5 2.0 pad_add_fusion
  25.5 2.1 broadcast_in_dim.79.weight_ref
  27.6 0.0 slice-done.1
  27.6 2.1 broadcast_in_dim.77.shift_ref
  29.7 10.8 %shard_map.109 = f32[3,256]{1,0:T(4,128)} custom-call(s32[3]{0:T(128)} %get-tuple-element.31.info_ref, f32[6144,128]{1,0:T(8,128)} %broadcast_in_dim.77.shift_ref, f32[6144,128]{1,0:T(8,128)} %broadcast_in_dim.79.weight_ref, f32[3,256]{1,0:T(4,128)} %reshape.83.place_ref, f32[3,256]{1,0:T(4,128)} %reshape.84.root_ref), custom_call_target="tpu_custom_call" | custom-call | flops 14155776000 | bytes 37748736 | tf_op jit(solution)/shard_map/pallas_call | solution.py:195
  40.5 0.0 slice-start
  40.5 1.3 pad_add_fusion.2.info_ref
  43.1 0.6 reshape.85.place_ref
  43.7 0.0 collective-permute-done
  43.8 0.8 fusion.30
  44.6 0.6 reshape.87.root_ref
  45.2 2.2 broadcast_in_dim.82.weight_ref
  47.4 0.0 slice-done
  47.4 2.2 broadcast_in_dim.81.shift_ref
  49.5 0.0 copy-start.1
  49.5 13.8 %shard_map.110 = f32[6,256]{1,0:T(8,128)} custom-call(s32[3]{0:T(128)} %get-tuple-element.30.info_ref, f32[6144,128]{1,0:T(8,128)} %broadcast_in_dim.81.shift_ref, f32[6144,128]{1,0:T(8,128)} %broadcast_in_dim.82.weight_ref, f32[6,256]{1,0:T(8,128)} %reshape.85.place_ref, f32[6,256]{1,0:T(8,128)} %reshape.87.root_ref), custom_call_target="tpu_custom_call" | custom-call | flops 28311552000 | bytes 75497472 | tf_op jit(solution)/shard_map/pallas_call | solution.py:195
  63.4 0.0 collective-permute-start.1
  64.0 0.0 copy-done.1
  64.1 0.6 sqrt.6.inverse_ref
  64.7 0.0 copy-done
  64.7 0.6 pad.9.order_ref
  65.3 1.3 stack.41.info_ref
  66.5 0.7 collective-permute-done.1
  67.2 1.3 add_rsqrt_fusion.inverse_ref
  68.5 12.0 %shard_map.111 = (bf16[32,3072]{1,0:T(8,128)(2,1)}, f32[16384,128]{1,0:T(8,128)}) custom-call(s32[2]{0:T(128)} %pad_add_fusion.2.info_ref, s32[16384]{0:T(1024)} %bitcast.62, bf16[32,16384]{1,0:T(8,128)(2,1)} %bitcast.58), custom_call_target="tpu_custom_call" | custom-call | tf_op jit(solution)/shard_map/pallas_call | solution.py:66
  80.5 21.3 %shard_map.112.rows_ref = bf16[128,6144]{1,0:T(8,128)(2,1)} custom-call(bf16[32,3072]{1,0:T(8,128)(2,1)} %get-tuple-element.15.source_ref), custom_call_target="tpu_custom_call" | custom-call | tf_op jit(solution)/shard_map/pallas_call | solution.py:319
  101.8 17.1 %shard_map.113 = bf16[128,768]{1,0:T(8,128)(2,1)} custom-call(s32[3]{0:T(128)} %get-tuple-element.31.info_ref, bf16[128,6144]{1,0:T(8,128)(2,1)} %shard_map.112.rows_ref, f32[6144,128]{1,0:T(8,128)} %broadcast_in_dim.77.shift_ref, f32[6144,128]{1,0:T(8,128)} %broadcast_in_dim.79.weight_ref, f32[3,256]{1,0:T(4,128)} %reshape.83.place_ref, ...), custom_call_target="tpu_custom_call" | custom-call | flops 14155776000 | tf_op jit(solution)/shard_map/pallas_call | solution.py:246
  119.0 8.1 %shard_map.114.level_ref = bf16[8,32,768]{2,1,0:T(8,128)(2,1)} custom-call(bf16[4,32,768]{2,1,0:T(8,128)(2,1)} %bitcast.63), custom_call_target="tpu_custom_call" | custom-call | tf_op jit(solution)/shard_map/pallas_call | solution.py:319
  127.1 20.5 %shard_map.115 = (bf16[32,3072]{1,0:T(8,128)(2,1)}, bf16[32,16384]{1,0:T(8,128)(2,1)}) custom-call(s32[5]{0:T(128)} %stack.41.info_ref, s32[16512]{0:T(1024)} %pad.9.order_ref, s32[16384]{0:T(1024)} %fusion.13.place_ref, bf16[8,32,768]{2,1,0:T(8,128)(2,1)} %shard_map.114.level_ref, f32[16384,128]{1,0:T(8,128)} %get-tuple-element.18.source_ref), custom_call_target="tpu_custom_call" | custom-call | tf_op jit(solution)/shard_map/pallas_call | solution.py:131
  147.6 1.8 reshape.92
  149.4 3.7 %constant_dynamic-slice_fusion = (bf16[32,1,8192]{2,1,0:T(2,128)(2,1)S(1)}, bf16[32,1,8192]{2,1,0:T(2,128)(2,1)S(1)}) fusion(bf16[32,2,8192]{2,1,0:T(2,128)(2,1)S(1)} %reshape.92, s32[]{:T(128)S(6)} %select_n.197, s32[]{:T(128)S(6)} %select_n.193), kind=kLoop, calls=%fused_computation.71 | loop fusion | bytes 2097160 | tf_op jit(solution)/shard_map/jit(dynamic_index_in_dim)/dynamic_slice | solution.py:344
  153.2 0.6 copy.33
  153.8 0.1 collective-permute-start.2
  153.8 30.6 %shard_map.116.rows_ref = bf16[128,6144]{1,0:T(8,128)(2,1)} custom-call(bf16[32,3072]{1,0:T(8,128)(2,1)} %get-tuple-element.19.source_ref), custom_call_target="tpu_custom_call" | custom-call | tf_op jit(solution)/shard_map/pallas_call | solution.py:319
  184.5 22.2 %shard_map.117 = bf16[128,1536]{1,0:T(8,128)(2,1)} custom-call(s32[3]{0:T(128)} %get-tuple-element.30.info_ref, bf16[128,6144]{1,0:T(8,128)(2,1)} %shard_map.116.rows_ref, f32[6144,128]{1,0:T(8,128)} %broadcast_in_dim.81.shift_ref, f32[6144,128]{1,0:T(8,128)} %broadcast_in_dim.82.weight_ref, f32[6,256]{1,0:T(8,128)} %reshape.85.place_ref, ...), custom_call_target="tpu_custom_call" | custom-call | flops 28311552000 | tf_op jit(solution)/shard_map/pallas_call | solution.py:246
  206.7 0.1 broadcast_in_dim.86
  206.7 0.6 fusion.2
  207.4 12.7 %shard_map.118 = bf16[8,32,1536]{2,1,0:T(8,128)(2,1)} custom-call(bf16[4,32,1536]{2,1,0:T(8,128)(2,1)} %bitcast.60), custom_call_target="tpu_custom_call" | custom-call | tf_op jit(solution)/shard_map/pallas_call | solution.py:319
  220.1 1.6 reshape.90
  221.7 0.9 copy.18
  222.7 0.3 copy.32
  223.0 0.0 collective-permute-done.2
  223.0 1.1 bitcast_dynamic-update-slice_fusion
  224.1 0.3 copy.26
  224.3 0.1 bitcast_bitcast_fusion
  224.4 1.1 copy.21
  225.5 0.8 reshape.94
  226.4 1.4 fusion.1
  (11 shorter events, 0.1 us)
Async XLA Ops:
  6.5 21.1 %slice-start.1 = ((f32[1,16384]{1,0:T(1,128)}), f32[1,6144]{1,0:T(1,128)S(1)}, s32[]{:S(2)}) async-start(f32[1,16384]{1,0:T(1,128)} %param.14), calls=%async_computation.2 | async-start | bytes 49152 | tf_op jit(solution)/shard_map/slice | solution.py:356
  6.5 62.0 %all-gather.3.cloned.1.call-start = ((), (), s32[]{:S(2)}) async-start(), calls=%async_computation | async-start | bytes 1572864 | tf_op jit(solution)/shard_map/all_gather | solution.py:419
  7.3 36.5 %collective-permute-start = (f32[6144]{0:T(1024)S(1)}, f32[6144]{0:T(1024)S(1)}, u32[]{:S(2)}, u32[]{:S(2)}) collective-permute-start(f32[6144]{0:T(1024)S(1)} %bitcast.68), channel_id=1, source_target_pairs={{0,8},{8,0},{16,24},{24,16},{1,9},{9,1},{17,25},{25,17},{2,10},{10... | collective-permute-start | bytes 73736 | tf_op jit(solution)/shard_map/ppermute | solution.py:395
  40.5 6.8 %slice-start = ((f32[1,16384]{1,0:T(1,128)}), f32[1,6144]{1,0:T(1,128)S(1)}, s32[]{:S(2)}) async-start(f32[1,16384]{1,0:T(1,128)} %param.19), calls=%async_computation.1 | async-start | bytes 49152 | tf_op jit(solution)/shard_map/slice | solution.py:356
  49.5 14.5 %copy-start.1 = (f32[3,256]{1,0:T(4,128)S(1)}, f32[3,256]{1,0:T(4,128)}, u32[]{:S(2)}) copy-start(f32[3,256]{1,0:T(4,128)} %shard_map.109) | copy-start | bytes 9220
  49.5 15.1 %copy-start = (s32[1,16384]{1,0:T(1,128)S(1)}, s32[1,16384]{1,0:T(1,128)}, u32[]{:S(2)}) copy-start(s32[1,16384]{1,0:T(1,128)} %param.18) | copy-start | bytes 196612
  63.4 3.9 %collective-permute-start.1 = (f32[6,256]{1,0:T(8,128)}, f32[6,256]{1,0:T(8,128)S(1)}, u32[]{:S(2)}, u32[]{:S(2)}) collective-permute-start(f32[6,256]{1,0:T(8,128)} %shard_map.110), channel_id=1, source_target_pairs={{0,8},{8,0},{16,24},{24,16},{1,9},{9,1},{17,25},{25,17},{2,10},{10... | collective-permute-start | bytes 18440 | tf_op jit(solution)/shard_map/ppermute | solution.py:415
  153.8 69.2 %collective-permute-start.2 = (bf16[32,8192]{1,0:T(8,128)(2,1)S(1)}, bf16[32,8192]{1,0:T(8,128)(2,1)}, u32[]{:S(2)}, u32[]{:S(2)}) collective-permute-start(bf16[32,8192]{1,0:T(8,128)(2,1)S(1)} %bitcast.59), channel_id=1, source_target_pairs={{0,1},{1,0},{2,3},{3,2},{4,5},{5,4},{6,7},{7,6},{8,9},{9,8},{10,11... | collective-permute-start | bytes 1572872 | tf_op jit(solution)/shard_map/ppermute | solution.py:347
Sparse Core Ops, SparseCore 0:
  10.5 22.4 all-gather.2
where the time goes:
time: 235 us
  Pallas kernels  169 us (72%)
  local copies, waits for them, and re-layouts  32.3 us (14%)
  between operations  18.3 us (8%)
  other arithmetic  11 us (5%)
  starting transfers between devices  3.1 us (1%)
    pallas_call x4, Pallas kernels, exchange(): pl.pallas_call(functools.partial(exchange_kernel, row_count, col_count, i...  72.7 us
    pallas_call x2, Pallas kernels, cauchy_product(): pl.pallas_call(functools.partial(apply_kernel, stride), out_shape=jax.Sha...  39.3 us
    pallas_call x2, Pallas kernels, column_norms(): pl.pallas_call(functools.partial(norm_kernel, stride), out_shape=jax.Shap...  24.6 us
    pallas_call x1, Pallas kernels, pick_two(): pl.pallas_call(functools.partial(pick_two_kernel, stride), out_shape=(jax...  20.5 us
    pallas_call x1, Pallas kernels, pick_one(): pl.pallas_call(pick_one_kernel, out_shape=(jax.ShapeDtypeStruct((rows, wi...  12 us
    broadcast_in_dim x4, local copies, waits for them, and re-layouts, spread_poles(): return jnp.broadcast_to(values[:, None], (limit, LANE))  8.57 us
  transfers between devices with their start and end apart: 4, of which 1 were waited for; matrix products, arithmetic and copies ran while one was open for 13% of the time, Pallas kernels for 38%

commit v1 on v0

--- a/solution.py
+++ b/solution.py
@@ -8,7 +8,8 @@
 from jax.sharding import PartitionSpec as P
 
 LANE = 128
-POLE_TILE = 512
+PART = 32
+POLE_TILE = 1024
 VMEM_LIMIT = 56 * 1024 * 1024
 MESH = pl.DeviceIdType.MESH
 
@@ -114,10 +115,12 @@
     lax.fori_loop(0, count, one, 0)
     offset, low, high = info_ref[2], info_ref[3], info_ref[4]
 
+    per_part = moved_ref.shape[2] // LANE
+
     def other(step, carry):
-        opening = pl.multiple_of(step * LANE, LANE)
+        opening = pl.multiple_of(lax.rem(step, per_part) * LANE, LANE)
         begin = offset + step * stride
-        moved_ref[:, pl.ds(opening, LANE)] = pick_block(
+        moved_ref[step // per_part, :, pl.ds(opening, LANE)] = pick_block(
             table_ref, stage_ref, lambda k: place_ref[order_ref[begin + k]], rows
         )
         return carry
@@ -125,14 +128,14 @@
     lax.fori_loop(low, high, other, 0)
 
 
-def pick_two(stride, info, order, place, level, table, width, moved_width):
+def pick_two(stride, info, order, place, level, table, width, moved_shape):
     group, rows, wide = level.shape
     wide = wide * group
     return pl.pallas_call(
         functools.partial(pick_two_kernel, stride),
         out_shape=(
             jax.ShapeDtypeStruct((rows, width), jnp.bfloat16),
-            jax.ShapeDtypeStruct((rows, moved_width), jnp.bfloat16),
+            jax.ShapeDtypeStruct(moved_shape, jnp.bfloat16),
         ),
         in_specs=[spec(pltpu.SMEM)] * 3 + [spec(pltpu.VMEM), spec(pl.ANY)],
         out_specs=(spec(pltpu.VMEM), spec(pltpu.VMEM)),
@@ -154,13 +157,16 @@
     return jnp.concatenate([values] * (width // LANE), axis=1)
 
 
-def quotients(start, rows, stride, half, shift_ref, weight_ref, place, root):
-    width = place.shape[1]
-    slot = lax.broadcasted_iota(jnp.int32, (rows, LANE), 0) + start
-    poles = across((slot * stride + half).astype(jnp.float32), width)
-    shifts = across(shift_ref[pl.ds(start, rows), :], width)
-    distance = (poles - place) + (shifts - root)
-    return across(weight_ref[pl.ds(start, rows), :], width) * inverse_of(distance)
+def offsets_from(place, stride, half):
+    steps = lax.broadcasted_iota(jnp.int32, (PART, place.shape[1]), 0) * stride + half
+    return steps.astype(jnp.float32) - place
+
+
+def quotients(start, stride, offsets, shift_ref, weight_ref, root):
+    width = root.shape[1]
+    shifts = across(shift_ref[pl.ds(start, PART), :], width)
+    distance = (offsets + (start * stride).astype(jnp.float32)) + (shifts - root)
+    return across(weight_ref[pl.ds(start, PART), :], width) * inverse_of(distance)
 
 
 def norm_kernel(stride, info_ref, shift_ref, weight_ref, place_ref, root_ref, out_ref):
@@ -171,16 +177,16 @@
     out_ref[...] = jnp.ones(out_ref.shape, jnp.float32)
 
     def one_block(block, carry):
-        place = place_ref[pl.ds(block, 1), :]
+        offsets = offsets_from(place_ref[pl.ds(block, 1), :], stride, half)
         root = root_ref[pl.ds(block, 1), :]
 
         def one_tile(tile, running):
             opening = pl.multiple_of(tile * POLE_TILE, POLE_TILE)
-            for part in range(POLE_TILE // 32):
+            for part in range(POLE_TILE // PART):
                 term = quotients(
-                    opening + part * 32, 32, stride, half, shift_ref, weight_ref, place, root
+                    opening + part * PART, stride, offsets, shift_ref, weight_ref, root
                 )
-                running = running + jnp.sum((term * term).reshape(4, 8, width), axis=0)
+                running = running + jnp.sum((term * term).reshape(PART // 8, 8, width), axis=0)
             return running
 
         sums = lax.fori_loop(0, tiles, one_tile, jnp.zeros((8, width), jnp.float32))
@@ -215,16 +221,16 @@
     out_ref[...] = jnp.zeros(out_ref.shape, out_ref.dtype)
 
     def one_block(block, carry):
-        place = place_ref[pl.ds(block, 1), :]
+        offsets = offsets_from(place_ref[pl.ds(block, 1), :], stride, half)
         root = root_ref[pl.ds(block, 1), :]
         inverse = inverse_ref[pl.ds(block, 1), :]
 
         def one_tile(tile, running):
             opening = pl.multiple_of(tile * POLE_TILE, POLE_TILE)
             pieces = []
-            for part in range(POLE_TILE // 32):
+            for part in range(POLE_TILE // PART):
                 term = quotients(
-                    opening + part * 32, 32, stride, half, shift_ref, weight_ref, place, root
+                    opening + part * PART, stride, offsets, shift_ref, weight_ref, root
                 )
                 pieces.append((term * inverse).astype(jnp.bfloat16))
             return running + jnp.dot(
@@ -269,9 +275,14 @@
     return jnp.maximum((total - member + group - 1) // group, 0)
 
 
-def exchange_kernel(
-    row_count, col_count, in_place, source_ref, out_ref, send_sem, recv_sem, own_sem
-):
+def greet(devices):
+    barrier = pltpu.get_barrier_semaphore()
+    for device in devices:
+        pl.semaphore_signal(barrier, inc=1, device_id=device, device_id_type=MESH)
+    pl.semaphore_wait(barrier, len(devices))
+
+
+def scatter_kernel(row_count, col_count, source_ref, out_ref, send_sem, recv_sem, own_sem):
     merge = lax.axis_index("merge")
     row, col = lax.axis_index("row"), lax.axis_index("col")
     group = row_count * col_count
@@ -280,23 +291,12 @@
     for k in range(1, group):
         peer = lax.rem(me + k, group)
         others.append((merge, peer // col_count, lax.rem(peer, col_count)))
-    barrier = pltpu.get_barrier_semaphore()
-    for device in others:
-        pl.semaphore_signal(barrier, inc=1, device_id=device, device_id_type=MESH)
-    pl.semaphore_wait(barrier, group - 1)
-    if in_place:
-        rows, width = source_ref.shape
-        target = out_ref.at[
-            pl.ds(pl.multiple_of(row * rows, rows), rows),
-            pl.ds(pl.multiple_of(col * width, width), width),
-        ]
-    else:
-        target = out_ref.at[me]
+    greet(others)
     copies = []
     for k, device in enumerate(others):
         copy = pltpu.make_async_remote_copy(
-            src_ref=source_ref if in_place else source_ref.at[device[1]],
-            dst_ref=target,
+            src_ref=source_ref.at[device[1]],
+            dst_ref=out_ref.at[me],
             send_sem=send_sem.at[k],
             recv_sem=recv_sem.at[k],
             device_id=device,
@@ -304,20 +304,70 @@
         )
         copy.start()
         copies.append(copy)
-    own = pltpu.make_async_copy(source_ref if in_place else source_ref.at[row], target, own_sem)
+    own = pltpu.make_async_copy(source_ref.at[row], out_ref.at[me], own_sem)
     own.start()
     own.wait()
     for copy in copies:
         copy.wait()
 
 
-def exchange(source, in_place, number):
+def gather_kernel(row_count, col_count, source_ref, out_ref, send_sem, recv_sem, own_sem):
+    merge = lax.axis_index("merge")
+    row, col = lax.axis_index("row"), lax.axis_index("col")
+    rows, width = source_ref.shape
+    parity = lax.rem(row, 2)
+    mate = (merge, row + 1 - 2 * parity, col)
+    count = row_count // 2 * col_count
+    me = row // 2 * col_count + col
+
+    def device_of(index):
+        return (merge, index // col_count * 2 + parity, lax.rem(index, col_count))
+
+    def place_of(device):
+        return out_ref.at[
+            pl.ds(pl.multiple_of(device[1] * rows, rows), rows),
+            pl.ds(pl.multiple_of(device[2] * width, width), width),
+        ]
+
+    def send(source, target, device, number):
+        copy = pltpu.make_async_remote_copy(
+            src_ref=source,
+            dst_ref=target,
+            send_sem=send_sem.at[number],
+            recv_sem=recv_sem.at[number],
+            device_id=device,
+            device_id_type=MESH,
+        )
+        copy.start()
+        return copy
+
+    others = [device_of(lax.rem(me + k, count)) for k in range(1, count)]
+    greet(others + [mate])
+    mine = place_of((merge, row, col))
+    far = [send(source_ref, mine, device, k) for k, device in enumerate(others)]
+    near = [send(source_ref, mine, mate, count - 1)]
+    own = pltpu.make_async_copy(source_ref, mine, own_sem)
+    own.start()
+    for k, copy in enumerate(far):
+        copy.wait_recv()
+        piece = place_of(device_of(lax.rem(me - (k + 1) + count, count)))
+        near.append(send(piece, piece, mate, count + k))
+    own.wait()
+    for copy in far:
+        copy.wait_send()
+    for copy in near:
+        copy.wait()
+
+
+def exchange(source, gathers, number):
     row_count, col_count = lax.axis_size("row"), lax.axis_size("col")
     group = row_count * col_count
     rows, width = source.shape[-2:]
-    shape = (row_count * rows, col_count * width) if in_place else (group, rows, width)
+    shape = (row_count * rows, col_count * width) if gathers else (group, rows, width)
     return pl.pallas_call(
-        functools.partial(exchange_kernel, row_count, col_count, in_place),
+        functools.partial(
+            gather_kernel if gathers else scatter_kernel, row_count, col_count
+        ),
         out_shape=jax.ShapeDtypeStruct(shape, source.dtype),
         in_specs=[spec(pl.ANY)],
         out_specs=spec(pl.ANY),
@@ -337,11 +387,10 @@
 
 def spread_moved(moved):
     col_count, col_index = lax.axis_size("col"), lax.axis_index("col")
-    rows, width = moved.shape
-    parts = moved.reshape(rows, col_count, width // col_count)
-    pieces = jnp.zeros((col_count, rows, width // col_count), moved.dtype)
+    rows, width = moved.shape[1], col_count * moved.shape[2]
+    pieces = jnp.zeros(moved.shape, moved.dtype)
     for k in range(col_count):
-        part = lax.dynamic_index_in_dim(parts, (col_index + k) % col_count, 1, keepdims=False)
+        part = lax.dynamic_index_in_dim(moved, (col_index + k) % col_count, 0, keepdims=False)
         if k:
             pairs = [(c, (c + k) % col_count) for c in range(col_count)]
             part = lax.ppermute(part, "col", pairs)
@@ -450,10 +499,12 @@
         [first, count_own, offset + col_index * LANE, low_turn, high_turn]
     ).astype(jnp.int32)
     order_pad = jnp.pad(order_two[0], (0, LANE))
+    moved_shape = (col_count, gathered.shape[0], out_width // col_count)
     picked, moved = pick_two(
-        col_count * LANE, info_pick, order_pad, place, level, table, share, out_width
+        col_count * LANE, info_pick, order_pad, place, level, table, share, moved_shape
     )
     rows_two = exchange(picked, True, 2)
+    rows_two, moved = lax.optimization_barrier((rows_two, moved))
     mixed = cauchy_product(
         2,
         info_two,

time: 235 us -> 194 us (0.83); the launches traced: 235 us -> 196 us
  Pallas kernels: 169 us -> 136 us
  local copies, waits for them, and re-layouts: 32.3 us -> 25.3 us
    pallas_call x4, Pallas kernels: 72.7 us -> 47.8 us  [exchange(): pl.pallas_call(functools.partial(gather_kernel if gathers else scatter_ke...]
    pallas_call x2, Pallas kernels: 39.3 us -> 32.1 us  [cauchy_product(): pl.pallas_call(functools.partial(apply_kernel, stride), out_shape=jax.Sha...]
    dynamic_slice x1 -> x0, local copies, waits for them, and re-layouts: 3.72 us -> none  [spread_moved(): lax.dynamic_index_in_dim(parts, (col_index + k) % col_count, 1, keepdims=...]
  transfers between devices with their start and end apart: 4 -> 4, of which waited for: 1 -> 1; matrix products, arithmetic and copies ran while one was open for 13% -> 16% of each run, Pallas kernels for 38% -> 28%
where the time goes in v1:
time: 194 us; the launch traced here: 196 us
  Pallas kernels  136 us (70%)
  local copies, waits for them, and re-layouts  25.3 us (13%)
  between operations  18.4 us (9%)
  other arithmetic  10.8 us (6%)
  starting transfers between devices  4.62 us (2%)
    pallas_call x4, Pallas kernels, exchange(): pl.pallas_call(functools.partial(gather_kernel if gathers else scatter_ke...  47.8 us
    pallas_call x2, Pallas kernels, cauchy_product(): pl.pallas_call(functools.partial(apply_kernel, stride), out_shape=jax.Sha...  32.1 us
    pallas_call x2, Pallas kernels, column_norms(): pl.pallas_call(functools.partial(norm_kernel, stride), out_shape=jax.Shap...  24 us
    pallas_call x1, Pallas kernels, pick_two(): pl.pallas_call(functools.partial(pick_two_kernel, stride), out_shape=(jax...  20.3 us
    pallas_call x1, Pallas kernels, pick_one(): pl.pallas_call(pick_one_kernel, out_shape=(jax.ShapeDtypeStruct((rows, wi...  12 us
    broadcast_in_dim x4, local copies, waits for them, and re-layouts, spread_poles(): return jnp.broadcast_to(values[:, None], (limit, LANE))  8.62 us
  transfers between devices with their start and end apart: 4, of which 1 were waited for; matrix products, arithmetic and copies ran while one was open for 16% of the time, Pallas kernels for 28%

profile of v1, /device:TPU:0, one launch (start us, length us, event | category | flops | bytes accessed | tf_op | source)
XLA Modules:
  0.0 196.0 jit_solution(15148879016037999931)
XLA Ops:
  6.5 0.0 slice-start.1
  6.5 0.0 all-gather.3.cloned.1.call-start
  6.5 0.8 slice.33
  7.3 3.0 %collective-permute-start = (f32[6144]{0:T(1024)S(1)}, f32[6144]{0:T(1024)S(1)}, u32[]{:S(2)}, u32[]{:S(2)}) collective-permute-start(f32[6144]{0:T(1024)S(1)} %bitcast.62), channel_id=1, source_target_pairs={{0,8},{8,0},{16,24},{24,16},{1,9},{9,1},{17,25},{25,17},{2,10},{10... | collective-permute-start | bytes 73736 | tf_op jit(solution)/shard_map/ppermute | solution.py:444
  10.3 0.0 all-gather.3.cloned.1.call-update
  10.4 1.3 dynamic_slice.42
  12.3 1.4 fusion.34
  15.8 0.7 slice.31
  16.5 0.7 slice.29
  17.3 0.6 reshape.80.root_ref
  17.9 0.6 reshape.79.place_ref
  18.5 0.7 slice.27
  19.2 0.6 fusion.30
  19.9 2.1 %fusion.12.place_ref = s32[16384]{0:T(1024)} fusion(s32[16384]{0:T(1024)} %bitcast.55, s32[]{:T(128)} %bitcast.9), kind=kLoop, calls=%fused_computation.30 | loop fusion | flops 622592 | bytes 131076 | tf_op jit(solution)/shard_map/jit(_where)/select_n | solution.py:491
  22.0 0.6 fusion.31
  22.6 0.7 select_convert_fusion
  23.4 1.9 pad_add_fusion
  25.3 2.1 %broadcast_in_dim.77.weight_ref = f32[6144,128]{1,0:T(8,128)} broadcast(f32[6144]{0:T(1024)S(1)} %fusion.30), dimensions={0} | broadcast | bytes 3170304 | tf_op jit(solution)/shard_map/broadcast_in_dim | solution.py:408
  27.4 0.0 slice-done.1
  27.4 2.1 %broadcast_in_dim.75.shift_ref = f32[6144,128]{1,0:T(8,128)} broadcast(f32[6144]{0:T(1024)S(1)} %bitcast.59), dimensions={0} | broadcast | bytes 3170304 | tf_op jit(solution)/shard_map/broadcast_in_dim | solution.py:408
  29.5 9.9 %shard_map.109 = f32[3,256]{1,0:T(4,128)} custom-call(s32[3]{0:T(128)} %get-tuple-element.35.info_ref, f32[6144,128]{1,0:T(8,128)} %broadcast_in_dim.75.shift_ref, f32[6144,128]{1,0:T(8,128)} %broadcast_in_dim.77.weight_ref, f32[3,256]{1,0:T(4,128)} %reshape.79.place_ref, f32[3,256]{1,0:T(4,128)} %reshape.80.root_ref), custom_call_target="tpu_custom_call" | custom-call | flops 14155776000 | bytes 37748736 | tf_op jit(solution)/shard_map/pallas_call | solution.py:201
  39.3 0.0 slice-start
  39.3 1.2 pad_add_fusion.2.info_ref
  41.9 0.6 reshape.81.place_ref
  42.5 0.0 collective-permute-done
  42.6 0.8 fusion.29
  43.4 0.6 reshape.83.root_ref
  44.0 2.2 %broadcast_in_dim.80.weight_ref = f32[6144,128]{1,0:T(8,128)} broadcast(f32[6144]{0:T(1024)S(1)} %fusion.31), dimensions={0} | broadcast | bytes 3170304 | tf_op jit(solution)/shard_map/broadcast_in_dim | solution.py:408
  46.2 0.0 slice-done
  46.2 2.2 %broadcast_in_dim.79.shift_ref = f32[6144,128]{1,0:T(8,128)} broadcast(f32[6144]{0:T(1024)S(1)} %bitcast.58), dimensions={0} | broadcast | bytes 3170304 | tf_op jit(solution)/shard_map/broadcast_in_dim | solution.py:408
  48.4 0.0 copy-start.2
  48.4 0.0 copy-start.1
  48.4 14.1 %shard_map.110 = f32[6,256]{1,0:T(8,128)} custom-call(s32[3]{0:T(128)} %get-tuple-element.34.info_ref, f32[6144,128]{1,0:T(8,128)} %broadcast_in_dim.79.shift_ref, f32[6144,128]{1,0:T(8,128)} %broadcast_in_dim.80.weight_ref, f32[6,256]{1,0:T(8,128)} %reshape.81.place_ref, f32[6,256]{1,0:T(8,128)} %reshape.83.root_ref), custom_call_target="tpu_custom_call" | custom-call | flops 28311552000 | bytes 75497472 | tf_op jit(solution)/shard_map/pallas_call | solution.py:201
  62.6 0.0 collective-permute-start.1
  63.2 0.0 copy-done.2
  63.2 0.6 sqrt.6.inverse_ref
  63.8 0.0 copy-done.1
  63.8 0.6 pad.9.order_ref
  64.5 1.2 stack.41.info_ref
  65.7 0.7 collective-permute-done.1
  66.4 1.3 add_rsqrt_fusion.inverse_ref
  67.7 0.0 all-gather.3.cloned.1.call-done
  67.7 12.0 %shard_map.111 = (bf16[32,3072]{1,0:T(8,128)(2,1)}, f32[16384,128]{1,0:T(8,128)}) custom-call(s32[2]{0:T(128)} %pad_add_fusion.2.info_ref, s32[16384]{0:T(1024)} %bitcast.56, bf16[32,16384]{1,0:T(8,128)(2,1)} %bitcast.53), custom_call_target="tpu_custom_call" | custom-call | tf_op jit(solution)/shard_map/pallas_call | solution.py:67
  79.7 13.2 %shard_map.112.rows_ref = bf16[128,6144]{1,0:T(8,128)(2,1)} custom-call(bf16[32,3072]{1,0:T(8,128)(2,1)} %get-tuple-element.17.source_ref), custom_call_target="tpu_custom_call" | custom-call | tf_op jit(solution)/shard_map/pallas_call | solution.py:367
  93.0 13.0 %shard_map.113 = bf16[128,768]{1,0:T(8,128)(2,1)} custom-call(s32[3]{0:T(128)} %get-tuple-element.35.info_ref, bf16[128,6144]{1,0:T(8,128)(2,1)} %shard_map.112.rows_ref, f32[6144,128]{1,0:T(8,128)} %broadcast_in_dim.75.shift_ref, f32[6144,128]{1,0:T(8,128)} %broadcast_in_dim.77.weight_ref, f32[3,256]{1,0:T(4,128)} %reshape.79.place_ref, ...), custom_call_target="tpu_custom_call" | custom-call | flops 14155776000 | tf_op jit(solution)/shard_map/pallas_call | solution.py:252
  106.0 8.5 %shard_map.114.level_ref = bf16[8,32,768]{2,1,0:T(8,128)(2,1)} custom-call(bf16[4,32,768]{2,1,0:T(8,128)(2,1)} %bitcast.57), custom_call_target="tpu_custom_call" | custom-call | tf_op jit(solution)/shard_map/pallas_call | solution.py:367
  114.5 20.3 %shard_map.115 = (bf16[32,3072]{1,0:T(8,128)(2,1)}, bf16[2,32,8192]{2,1,0:T(8,128)(2,1)}) custom-call(s32[5]{0:T(128)} %stack.41.info_ref, s32[16512]{0:T(1024)} %pad.9.order_ref, s32[16384]{0:T(1024)} %fusion.12.place_ref, bf16[8,32,768]{2,1,0:T(8,128)(2,1)} %shard_map.114.level_ref, f32[16384,128]{1,0:T(8,128)} %get-tuple-element.20.source_ref), custom_call_target="tpu_custom_call" | custom-call | tf_op jit(solution)/shard_map/pallas_call | solution.py:134
  134.8 0.0 copy-start
  134.8 13.5 %shard_map.116.rows_ref = bf16[128,6144]{1,0:T(8,128)(2,1)} custom-call(bf16[32,3072]{1,0:T(8,128)(2,1)} %get-tuple-element.21.source_ref), custom_call_target="tpu_custom_call" | custom-call | tf_op jit(solution)/shard_map/pallas_call | solution.py:367
  148.4 0.1 broadcast_in_dim.84
  148.5 0.0 copy-done
  148.5 0.9 dynamic-slice_bitcast_fusion
  149.3 1.6 collective-permute-start.2
  150.9 19.1 %shard_map.117 = bf16[128,1536]{1,0:T(8,128)(2,1)} custom-call(s32[3]{0:T(128)} %get-tuple-element.34.info_ref, bf16[128,6144]{1,0:T(8,128)(2,1)} %shard_map.116.rows_ref, f32[6144,128]{1,0:T(8,128)} %broadcast_in_dim.79.shift_ref, f32[6144,128]{1,0:T(8,128)} %broadcast_in_dim.80.weight_ref, f32[6,256]{1,0:T(8,128)} %reshape.81.place_ref, ...), custom_call_target="tpu_custom_call" | custom-call | flops 28311552000 | tf_op jit(solution)/shard_map/pallas_call | solution.py:252
  170.0 12.5 %shard_map.118 = bf16[8,32,1536]{2,1,0:T(8,128)(2,1)} custom-call(bf16[4,32,1536]{2,1,0:T(8,128)(2,1)} %bitcast.54), custom_call_target="tpu_custom_call" | custom-call | tf_op jit(solution)/shard_map/pallas_call | solution.py:367
  182.5 1.6 reshape.86
  184.2 0.9 copy.16
  185.1 0.3 copy.22
  185.4 0.0 collective-permute-done.2
  185.5 0.3 copy.20
  185.7 0.1 bitcast_bitcast_fusion
  185.8 1.1 copy.17
  186.9 0.8 reshape.89
  187.7 1.4 fusion.1
  (10 shorter events, 0.2 us)
Async XLA Ops:
  6.5 20.8 %slice-start.1 = ((f32[1,16384]{1,0:T(1,128)}), f32[1,6144]{1,0:T(1,128)S(1)}, s32[]{:S(2)}) async-start(f32[1,16384]{1,0:T(1,128)} %param.14), calls=%async_computation.2 | async-start | bytes 49152 | tf_op jit(solution)/shard_map/slice | solution.py:405
  6.5 61.2 %all-gather.3.cloned.1.call-start = ((), (), s32[]{:S(2)}) async-start(), calls=%async_computation | async-start | bytes 1572864 | tf_op jit(solution)/shard_map/all_gather | solution.py:468
  7.3 35.2 %collective-permute-start = (f32[6144]{0:T(1024)S(1)}, f32[6144]{0:T(1024)S(1)}, u32[]{:S(2)}, u32[]{:S(2)}) collective-permute-start(f32[6144]{0:T(1024)S(1)} %bitcast.62), channel_id=1, source_target_pairs={{0,8},{8,0},{16,24},{24,16},{1,9},{9,1},{17,25},{25,17},{2,10},{10... | collective-permute-start | bytes 73736 | tf_op jit(solution)/shard_map/ppermute | solution.py:444
  39.3 6.9 %slice-start = ((f32[1,16384]{1,0:T(1,128)}), f32[1,6144]{1,0:T(1,128)S(1)}, s32[]{:S(2)}) async-start(f32[1,16384]{1,0:T(1,128)} %param.19), calls=%async_computation.1 | async-start | bytes 49152 | tf_op jit(solution)/shard_map/slice | solution.py:405
  48.4 14.8 %copy-start.2 = (f32[3,256]{1,0:T(4,128)S(1)}, f32[3,256]{1,0:T(4,128)}, u32[]{:S(2)}) copy-start(f32[3,256]{1,0:T(4,128)} %shard_map.109) | copy-start | bytes 9220
  48.4 15.4 %copy-start.1 = (s32[1,16384]{1,0:T(1,128)S(1)}, s32[1,16384]{1,0:T(1,128)}, u32[]{:S(2)}) copy-start(s32[1,16384]{1,0:T(1,128)} %param.18) | copy-start | bytes 196612
  62.6 3.9 %collective-permute-start.1 = (f32[6,256]{1,0:T(8,128)}, f32[6,256]{1,0:T(8,128)S(1)}, u32[]{:S(2)}, u32[]{:S(2)}) collective-permute-start(f32[6,256]{1,0:T(8,128)} %shard_map.110), channel_id=1, source_target_pairs={{0,8},{8,0},{16,24},{24,16},{1,9},{9,1},{17,25},{25,17},{2,10},{10... | collective-permute-start | bytes 18440 | tf_op jit(solution)/shard_map/ppermute | solution.py:464
  134.8 13.6 %copy-start = (bf16[2,32,8192]{2,1,0:T(8,128)(2,1)S(1)}, bf16[2,32,8192]{2,1,0:T(8,128)(2,1)}, u32[]{:S(2)}) copy-start(bf16[2,32,8192]{2,1,0:T(8,128)(2,1)} %get-tuple-element.26) | copy-start | bytes 3145732
  149.3 36.0 %collective-permute-start.2 = (bf16[32,8192]{1,0:T(8,128)(2,1)}, bf16[32,8192]{1,0:T(8,128)(2,1)S(1)}, u32[]{:S(2)}, u32[]{:S(2)}) collective-permute-start(bf16[32,8192]{1,0:T(8,128)(2,1)} %get-tuple-element.27), channel_id=1, source_target_pairs={{0,1},{1,0},{2,3},{3,2},{4,5},{5,4},{6,7},{7,6},{8,9},{9,8},{10,11... | collective-permute-start | bytes 1572872 | tf_op jit(solution)/shard_map/ppermute | solution.py:396
Sparse Core Ops, SparseCore 0:
  10.5 22.4 all-gather.2

commit v2 on v1

--- a/solution.py
+++ b/solution.py
@@ -378,6 +378,14 @@
         ],
         compiler_params=pltpu.CompilerParams(collective_id=number, has_side_effects=True),
     )(source)
+
+
+def join_rows(piece):
+    rows, width = piece.shape
+    row_count, col_count = lax.axis_size("row"), lax.axis_size("col")
+    parts = lax.all_gather(piece, ("row", "col"), axis=0, tiled=False)
+    parts = parts.reshape(row_count, col_count, rows, width)
+    return jnp.transpose(parts, (0, 2, 1, 3)).reshape(row_count * rows, col_count * width)
 
 
 def join_columns(piece, number):
@@ -475,11 +483,14 @@
     sums_one = column_norms(1, info_one, shift_one, weight_one, place_one, root_one)
     inverse_one = 1.0 / jnp.sqrt(sums_one)
     inverse_two = 1.0 / jnp.sqrt(sums_two)
-    gathered, inverse_one, inverse_two, weight_one, weight_two = lax.optimization_barrier(
-        (gathered, inverse_one, inverse_two, weight_one, weight_two)
+    gathered, inverse_one, weight_one = lax.optimization_barrier(
+        (gathered, inverse_one, weight_one)
     )
     picked, table = pick_one(jnp.stack([first, live]).astype(jnp.int32), order_one[0], gathered, share)
-    rows_one = exchange(picked, True, 0)
+    rows_one = join_rows(picked)
+    rows_one, inverse_two, weight_two = lax.optimization_barrier(
+        (rows_one, inverse_two, weight_two)
+    )
     level = cauchy_product(
         1, info_one, rows_one, shift_one, weight_one, place_one, root_one, inverse_one
     )

time: 194 us -> 194 us (level); the launches traced: 196 us -> 193 us
  Pallas kernels: 136 us -> 128 us
  local copies, waits for them, and re-layouts: 25.3 us -> 30.6 us
    pallas_call x4 -> x3, Pallas kernels: 47.8 us -> 33.8 us  [exchange(): pl.pallas_call(functools.partial(gather_kernel if gathers else scatter_ke...]
    pallas_call x2, Pallas kernels: 32.1 us -> 35.3 us  [cauchy_product(): pl.pallas_call(functools.partial(apply_kernel, stride), out_shape=jax.Sha...]
    reshape x0 -> x1, local copies, waits for them, and re-layouts: none -> 3.03 us  [join_rows(): parts = parts.reshape(row_count, col_count, rows, width)]
    pallas_call x2, Pallas kernels: 24 us -> 26.3 us  [column_norms(): pl.pallas_call(functools.partial(norm_kernel, stride), out_shape=jax.Shap...]
  transfers between devices with their start and end apart: 4 -> 5, of which waited for: 1 -> 1; matrix products, arithmetic and copies ran while one was open for 16% -> 16% of each run, Pallas kernels for 28% -> 31%
where the time goes in v2:
time: 194 us; the launch traced here: 193 us
  Pallas kernels  128 us (66%)
  local copies, waits for them, and re-layouts  30.6 us (16%)
  between operations  18.4 us (9%)
  other arithmetic  9.6 us (5%)
  starting transfers between devices  4.72 us (2%)
  waiting for transfers between devices  1.94 us (1%)
    pallas_call x2, Pallas kernels, cauchy_product(): pl.pallas_call(functools.partial(apply_kernel, stride), out_shape=jax.Sha...  35.3 us
    pallas_call x3, Pallas kernels, exchange(): pl.pallas_call(functools.partial(gather_kernel if gathers else scatter_ke...  33.8 us
    pallas_call x2, Pallas kernels, column_norms(): pl.pallas_call(functools.partial(norm_kernel, stride), out_shape=jax.Shap...  26.3 us
    pallas_call x1, Pallas kernels, pick_two(): pl.pallas_call(functools.partial(pick_two_kernel, stride), out_shape=(jax...  20.7 us
    pallas_call x1, Pallas kernels, pick_one(): pl.pallas_call(pick_one_kernel, out_shape=(jax.ShapeDtypeStruct((rows, wi...  12 us
    broadcast_in_dim x4, local copies, waits for them, and re-layouts, spread_poles(): return jnp.broadcast_to(values[:, None], (limit, LANE))  8.66 us
  transfers between devices with their start and end apart: 5, of which 1 were waited for; matrix products, arithmetic and copies ran while one was open for 16% of the time, Pallas kernels for 31%

profile of v2, /device:TPU:0, one launch (start us, length us, event | category | flops | bytes accessed | tf_op | source)
XLA Modules:
  0.0 193.3 jit_solution(13619705471642381249)
XLA Ops:
  6.5 0.0 slice-start.1
  6.5 0.0 all-gather.5.cloned.1.call-start
  6.5 0.7 all-gather.5.cloned.1.call-update
  7.3 0.0 all-gather.7.cloned.1.call-start
  7.3 0.7 slice.33
  8.0 3.0 %collective-permute-start = (f32[6144]{0:T(1024)S(1)}, f32[6144]{0:T(1024)S(1)}, u32[]{:S(2)}, u32[]{:S(2)}) collective-permute-start(f32[6144]{0:T(1024)S(1)} %bitcast.70), channel_id=1, source_target_pairs={{0,8},{8,0},{16,24},{24,16},{1,9},{9,1},{17,25},{25,17},{2,10},{10... | collective-permute-start | bytes 73736 | tf_op jit(solution)/shard_map/ppermute | solution.py:452
  11.1 1.2 dynamic_slice.42
  12.9 1.4 fusion.34
  16.4 0.7 slice.29
  17.2 0.6 reshape.86.root_ref
  17.8 0.6 reshape.85.place_ref
  18.4 0.7 slice.27
  19.2 0.6 fusion.30
  19.7 0.7 slice.31
  20.5 0.7 fusion.31
  21.2 1.8 pad_add_fusion
  23.0 2.1 %broadcast_in_dim.77.weight_ref = f32[6144,128]{1,0:T(8,128)} broadcast(f32[6144]{0:T(1024)S(1)} %fusion.30), dimensions={0} | broadcast | bytes 3170304 | tf_op jit(solution)/shard_map/broadcast_in_dim | solution.py:416
  25.1 0.0 slice-done.1
  25.1 2.1 %broadcast_in_dim.75.shift_ref = f32[6144,128]{1,0:T(8,128)} broadcast(f32[6144]{0:T(1024)S(1)} %bitcast.67), dimensions={0} | broadcast | bytes 3170304 | tf_op jit(solution)/shard_map/broadcast_in_dim | solution.py:416
  27.3 0.0 copy-start.1
  27.3 9.9 %shard_map.109 = f32[3,256]{1,0:T(4,128)} custom-call(s32[3]{0:T(128)} %get-tuple-element.37.info_ref, f32[6144,128]{1,0:T(8,128)} %broadcast_in_dim.75.shift_ref, f32[6144,128]{1,0:T(8,128)} %broadcast_in_dim.77.weight_ref, f32[3,256]{1,0:T(4,128)} %reshape.85.place_ref, f32[3,256]{1,0:T(4,128)} %reshape.86.root_ref), custom_call_target="tpu_custom_call" | custom-call | flops 14155776000 | bytes 37748736 | tf_op jit(solution)/shard_map/pallas_call | solution.py:201
  37.2 0.6 select_convert_fusion
  37.8 0.0 copy-done.1
  37.8 1.2 fusion.12.place_ref
  39.0 1.1 pad_add_fusion.2.info_ref
  40.2 1.3 sqrt.6.inverse_ref
  42.7 0.6 reshape.89.place_ref
  43.3 0.0 collective-permute-done
  43.4 0.8 fusion.29
  44.2 0.6 reshape.91.root_ref
  44.8 12.0 %shard_map.110 = (bf16[32,3072]{1,0:T(8,128)(2,1)}, f32[16384,128]{1,0:T(8,128)}) custom-call(s32[2]{0:T(128)} %pad_add_fusion.2.info_ref, s32[16384]{0:T(1024)} %bitcast.63, bf16[32,16384]{1,0:T(8,128)(2,1)} %bitcast.61), custom_call_target="tpu_custom_call" | custom-call | tf_op jit(solution)/shard_map/pallas_call | solution.py:67
  56.8 0.0 all-gather.7.cloned.1.call-update
  56.8 2.2 %broadcast_in_dim.80.weight_ref = f32[6144,128]{1,0:T(8,128)} broadcast(f32[6144]{0:T(1024)S(1)} %fusion.31), dimensions={0} | broadcast | bytes 3170304 | tf_op jit(solution)/shard_map/broadcast_in_dim | solution.py:416
  59.0 0.0 slice-done
  59.0 2.2 %broadcast_in_dim.79.shift_ref = f32[6144,128]{1,0:T(8,128)} broadcast(f32[6144]{0:T(1024)S(1)} %bitcast.66), dimensions={0} | broadcast | bytes 3170304 | tf_op jit(solution)/shard_map/broadcast_in_dim | solution.py:416
  61.2 16.4 %shard_map.111 = f32[6,256]{1,0:T(8,128)} custom-call(s32[3]{0:T(128)} %get-tuple-element.36.info_ref, f32[6144,128]{1,0:T(8,128)} %broadcast_in_dim.79.shift_ref, f32[6144,128]{1,0:T(8,128)} %broadcast_in_dim.80.weight_ref, f32[6,256]{1,0:T(8,128)} %reshape.89.place_ref, f32[6,256]{1,0:T(8,128)} %reshape.91.root_ref), custom_call_target="tpu_custom_call" | custom-call | flops 28311552000 | bytes 75497472 | tf_op jit(solution)/shard_map/pallas_call | solution.py:201
  77.6 0.0 collective-permute-start.1
  78.4 0.0 copy-done.2
  78.4 0.6 pad.9.order_ref
  79.0 1.3 stack.41.info_ref
  80.3 1.2 collective-permute-done.1
  81.5 1.3 add_rsqrt_fusion.inverse_ref
  82.8 3.0 %copy.18 = bf16[4,2,32,3072]{3,1,2,0:T(2,128)(2,1)S(1)} copy(bf16[4,2,32,3072]{3,2,1,0:T(8,128)(2,1)} %bitcast.59) | data formatting | bytes 3145728 | tf_op jit(solution)/shard_map/reshape | solution.py:387
  85.8 1.6 copy.22
  87.4 13.0 %shard_map.112 = bf16[128,768]{1,0:T(8,128)(2,1)} custom-call(s32[3]{0:T(128)} %get-tuple-element.37.info_ref, bf16[128,6144]{1,0:T(8,128)(2,1)} %bitcast.60, f32[6144,128]{1,0:T(8,128)} %broadcast_in_dim.75.shift_ref, f32[6144,128]{1,0:T(8,128)} %broadcast_in_dim.77.weight_ref, f32[3,256]{1,0:T(4,128)} %reshape.85.place_ref, f32[3,256]{1,0:T(4,128)} %reshape.86.root_ref, ...), custom_call_target="tpu_custom_call" | custom-call | flops 14155776000 | tf_op jit(solution)/shard_map/pallas_call | solution.py:252
  100.4 8.6 %shard_map.113.level_ref = bf16[8,32,768]{2,1,0:T(8,128)(2,1)} custom-call(bf16[4,32,768]{2,1,0:T(8,128)(2,1)} %bitcast.65), custom_call_target="tpu_custom_call" | custom-call | tf_op jit(solution)/shard_map/pallas_call | solution.py:367
  109.0 20.7 %shard_map.114 = (bf16[32,3072]{1,0:T(8,128)(2,1)}, bf16[2,32,8192]{2,1,0:T(8,128)(2,1)}) custom-call(s32[5]{0:T(128)} %stack.41.info_ref, s32[16512]{0:T(1024)} %pad.9.order_ref, s32[16384]{0:T(1024)} %fusion.12.place_ref, bf16[8,32,768]{2,1,0:T(8,128)(2,1)} %shard_map.113.level_ref, f32[16384,128]{1,0:T(8,128)} %get-tuple-element.22.source_ref), custom_call_target="tpu_custom_call" | custom-call | tf_op jit(solution)/shard_map/pallas_call | solution.py:134
  129.8 0.0 copy-start
  129.8 13.2 %shard_map.115.rows_ref = bf16[128,6144]{1,0:T(8,128)(2,1)} custom-call(bf16[32,3072]{1,0:T(8,128)(2,1)} %get-tuple-element.23.source_ref), custom_call_target="tpu_custom_call" | custom-call | tf_op jit(solution)/shard_map/pallas_call | solution.py:367
  143.0 0.1 broadcast_in_dim.84
  143.0 0.0 copy-done
  143.0 0.9 dynamic-slice_bitcast_fusion
  143.9 1.7 collective-permute-start.2
  145.6 22.3 %shard_map.116 = bf16[128,1536]{1,0:T(8,128)(2,1)} custom-call(s32[3]{0:T(128)} %get-tuple-element.36.info_ref, bf16[128,6144]{1,0:T(8,128)(2,1)} %shard_map.115.rows_ref, f32[6144,128]{1,0:T(8,128)} %broadcast_in_dim.79.shift_ref, f32[6144,128]{1,0:T(8,128)} %broadcast_in_dim.80.weight_ref, f32[6,256]{1,0:T(8,128)} %reshape.89.place_ref, ...), custom_call_target="tpu_custom_call" | custom-call | flops 28311552000 | tf_op jit(solution)/shard_map/pallas_call | solution.py:252
  167.8 12.0 %shard_map.117 = bf16[8,32,1536]{2,1,0:T(8,128)(2,1)} custom-call(bf16[4,32,1536]{2,1,0:T(8,128)(2,1)} %bitcast.62), custom_call_target="tpu_custom_call" | custom-call | tf_op jit(solution)/shard_map/pallas_call | solution.py:367
  179.8 1.6 reshape.94
  181.5 0.9 copy.19
  182.4 0.3 copy.26
  182.7 0.0 collective-permute-done.2
  182.8 0.3 copy.24
  183.0 0.1 bitcast_bitcast_fusion
  183.1 1.1 copy.20
  184.2 0.8 reshape.97
  185.0 1.4 fusion.1
  (14 shorter events, 0.2 us)
Async XLA Ops:
  6.5 18.6 %slice-start.1 = ((f32[1,16384]{1,0:T(1,128)}), f32[1,6144]{1,0:T(1,128)S(1)}, s32[]{:S(2)}) async-start(f32[1,16384]{1,0:T(1,128)} %param.14), calls=%async_computation.3 | async-start | bytes 49152 | tf_op jit(solution)/shard_map/slice | solution.py:413
  6.5 38.2 %all-gather.5.cloned.1.call-start = ((), (), s32[]{:S(2)}) async-start(), calls=%async_computation | async-start | bytes 1572864 | tf_op jit(solution)/shard_map/all_gather | solution.py:476
  7.3 75.5 %all-gather.7.cloned.1.call-start = ((), (), s32[]{:S(2)}) async-start(), calls=%async_computation.1 | async-start | bytes 1769472 | tf_op jit(solution)/shard_map/all_gather | solution.py:386
  8.0 35.3 %collective-permute-start = (f32[6144]{0:T(1024)S(1)}, f32[6144]{0:T(1024)S(1)}, u32[]{:S(2)}, u32[]{:S(2)}) collective-permute-start(f32[6144]{0:T(1024)S(1)} %bitcast.70), channel_id=1, source_target_pairs={{0,8},{8,0},{16,24},{24,16},{1,9},{9,1},{17,25},{25,17},{2,10},{10... | collective-permute-start | bytes 73736 | tf_op jit(solution)/shard_map/ppermute | solution.py:452
  27.3 10.6 %copy-start.1 = (s32[1,16384]{1,0:T(1,128)S(1)}, s32[1,16384]{1,0:T(1,128)}, u32[]{:S(2)}) copy-start(s32[1,16384]{1,0:T(1,128)} %param.13) | copy-start | bytes 196612
  37.1 21.9 %slice-start = ((f32[1,16384]{1,0:T(1,128)}), f32[1,6144]{1,0:T(1,128)S(1)}, s32[]{:S(2)}) async-start(f32[1,16384]{1,0:T(1,128)} %param.19), calls=%async_computation.2 | async-start | bytes 49152 | tf_op jit(solution)/shard_map/slice | solution.py:413
  61.2 17.2 %copy-start.2 = (s32[1,16384]{1,0:T(1,128)S(1)}, s32[1,16384]{1,0:T(1,128)}, u32[]{:S(2)}) copy-start(s32[1,16384]{1,0:T(1,128)} %param.18) | copy-start | bytes 196612
  77.6 3.9 %collective-permute-start.1 = (f32[6,256]{1,0:T(8,128)}, f32[6,256]{1,0:T(8,128)S(1)}, u32[]{:S(2)}, u32[]{:S(2)}) collective-permute-start(f32[6,256]{1,0:T(8,128)} %shard_map.111), channel_id=1, source_target_pairs={{0,8},{8,0},{16,24},{24,16},{1,9},{9,1},{17,25},{25,17},{2,10},{10... | collective-permute-start | bytes 18440 | tf_op jit(solution)/shard_map/ppermute | solution.py:472
  129.8 13.3 %copy-start = (bf16[2,32,8192]{2,1,0:T(8,128)(2,1)S(1)}, bf16[2,32,8192]{2,1,0:T(8,128)(2,1)}, u32[]{:S(2)}) copy-start(bf16[2,32,8192]{2,1,0:T(8,128)(2,1)} %get-tuple-element.28) | copy-start | bytes 3145732
  143.9 38.8 %collective-permute-start.2 = (bf16[32,8192]{1,0:T(8,128)(2,1)}, bf16[32,8192]{1,0:T(8,128)(2,1)S(1)}, u32[]{:S(2)}, u32[]{:S(2)}) collective-permute-start(bf16[32,8192]{1,0:T(8,128)(2,1)} %get-tuple-element.29), channel_id=1, source_target_pairs={{0,1},{1,0},{2,3},{3,2},{4,5},{5,4},{6,7},{7,6},{8,9},{9,8},{10,11... | collective-permute-start | bytes 1572872 | tf_op jit(solution)/shard_map/ppermute | solution.py:404
Sparse Core Ops, SparseCore 0:
  8.9 23.9 all-gather.4
  56.9 23.7 all-gather.6
